TPU v7x, 32 devices: a whole 2x2x4 slice. The times are simulated.
32 devices in a mesh: seq: 2 (over y), head: 4 (over x, core), ctx: 4 (over z).
Axes of the slice: x: 2, y: 2, z: 4, core: 2. Of those that a mesh axis runs over, the one named last changes fastest.
Arguments:
- q_new: bfloat16 [1024, 8192], P('seq', ('head', 'ctx')), may hold values from -6 to 6
- k_prefix: bfloat16 [1024, 1024], P('seq', 'head'), may hold values from -204 to 204
- v_prefix: bfloat16 [1024, 1024], P('seq', 'head'), may hold values from -6 to 6
- k_new: bfloat16 [1024, 1024], P('seq', 'head'), may hold values from -204 to 204
- v_new: bfloat16 [1024, 1024], P('seq', 'head'), may hold values from -6 to 6
- block_offsets: int32 [8], P('seq'), may hold values from 0 to 511
- dec_hidden: bfloat16 [256, 8192], P(None, 'ctx'), may hold values from -6 to 6
- w_query: bfloat16 [8192, 4, 2048], P('ctx', 'head', 'seq'), may hold values from -0.0625 to 0.0625
- w_out: bfloat16 [4, 2048, 8192], P('head', 'seq', 'ctx'), may hold values from -0.0625 to 0.0625
- k_own: bfloat16 [256, 1024], P(None, 'head'), may hold values from -21 to 21
- v_own: bfloat16 [256, 1024], P(None, 'head'), may hold values from -6 to 6
- valid_len: int32 [256], replicated, may hold values from 1 to 1024
- parent: int32 [256], replicated, may hold values from 0 to 1023
Outputs:
- prefill_out: bfloat16 [1024, 8192], P('seq', ('head', 'ctx'))
- decoded: bfloat16 [256, 8192], P(('seq', 'head'), 'ctx')
All inputs are finite; a program needn't handle non-finite values.
Results may differ from a plain program's by a relative error of at most 0.017.
The roundings to bfloat16 on the way count: a program that leaves them out, or rounds other values in their place, can miss the bound.
Values may be sent and summed in bfloat16 or wider, within the bound.
A program may use at most 64 MiB of HBM per device.

v0:
```python
import math

import jax
import jax.numpy as jnp
from jax import lax
from jax.sharding import PartitionSpec as P

HQ = 64
KVH = 8
HD = 128
QBLK = 128


NEG_FILL = -1e30


def spread(shard, axis, root):
    mine = lax.axis_index(axis) == root
    return lax.psum(jnp.where(mine, shard, jnp.zeros_like(shard)), axis)


def joined(part, axis, combine):
    gathered = jax.tree.map(lambda a: lax.all_gather(a, axis), part)

    def take(source):
        return jax.tree.map(lambda a: lax.dynamic_index_in_dim(a, source, 0, False), gathered)

    return lax.fori_loop(
        1, lax.axis_size(axis), lambda source, state: combine(state, take(source)), take(0)
    )


def online_update(carry, queries, keys, values, visible, scale):
    best, total, accum = carry
    scores = jnp.einsum("qd,kd->qk", queries, keys, preferred_element_type=jnp.float32) * scale
    scores = jnp.where(visible, scores, NEG_FILL)
    fresh = jnp.maximum(best, jnp.max(scores, axis=1))
    factor = jnp.exp(best - fresh)
    weights = jnp.where(visible, jnp.exp(scores - fresh[:, None]), 0.0)
    total = total * factor + jnp.sum(weights, axis=1)
    accum = accum * factor[:, None] + jnp.dot(
        weights.astype(jnp.bfloat16), values, preferred_element_type=jnp.float32
    )
    return (fresh, total, accum)


def combine_parts(left, right):
    best = jnp.maximum(left[0], right[0])
    left_f = jnp.exp(left[0] - best)
    right_f = jnp.exp(right[0] - best)
    return (
        best,
        left[1] * left_f + right[1] * right_f,
        left[2] * left_f[:, None] + right[2] * right_f[:, None],
    )


def body(
    q_new,
    k_prefix,
    v_prefix,
    k_new,
    v_new,
    block_offsets,
    dec_hidden,
    w_query,
    w_out,
    k_own,
    v_own,
    valid_len,
    parent,
):
    group_size = HQ // KVH
    scale = 1.0 / math.sqrt(HD)
    n_seq = lax.axis_size("seq")
    seq_idx = lax.axis_index("seq")
    ctx_idx = lax.axis_index("ctx")
    block = q_new.shape[0]
    per_dev = q_new.shape[1] // HD
    prefix_len = block * n_seq
    kv_pre = ctx_idx * per_dev // group_size
    queries = q_new.reshape(block * per_dev, HD)
    first_rows = jnp.repeat(block_offsets, QBLK * per_dev)
    qpos_rows = seq_idx * block + jnp.arange(block * per_dev, dtype=jnp.int32) // per_dev

    def head_cols(arr, which):
        return lax.dynamic_slice_in_dim(arr, which * HD, HD, arr.ndim - 1)

    init = (
        jnp.full((block * per_dev,), NEG_FILL, jnp.float32),
        jnp.zeros((block * per_dev,), jnp.float32),
        jnp.zeros((block * per_dev, HD), jnp.float32),
    )
    spans = (
        head_cols(k_prefix, kv_pre),
        head_cols(v_prefix, kv_pre),
        head_cols(k_new, kv_pre),
        head_cols(v_new, kv_pre),
    )
    carry = init
    kp = lax.all_gather(spans[0], "seq", axis=0, tiled=True)
    vp = lax.all_gather(spans[1], "seq", axis=0, tiled=True)
    kn = lax.all_gather(spans[2], "seq", axis=0, tiled=True)
    vn = lax.all_gather(spans[3], "seq", axis=0, tiled=True)
    rows = kp.shape[0]
    step_len = math.gcd(rows, 512)
    count = rows // step_len

    def one(state, items):
        kpb, vpb, knb, vnb, base = items
        pos = base + jnp.arange(step_len, dtype=jnp.int32)
        state = online_update(state, queries, kpb, vpb, pos[None, :] >= first_rows[:, None], scale)
        state = online_update(state, queries, knb, vnb, pos[None, :] <= qpos_rows[:, None], scale)
        return (state, None)

    bases = step_len * jnp.arange(count, dtype=jnp.int32)
    carry, _ = lax.scan(
        one,
        carry,
        (
            kp.reshape(count, step_len, HD),
            vp.reshape(count, step_len, HD),
            kn.reshape(count, step_len, HD),
            vn.reshape(count, step_len, HD),
            bases,
        ),
    )
    best, total, accum = carry
    prefill_out = (accum / total[:, None]).astype(jnp.bfloat16).reshape(block, per_dev * HD)
    partial_q = jnp.dot(
        dec_hidden, w_query.reshape(w_query.shape[0], -1), preferred_element_type=jnp.float32
    )
    dec_q = lax.psum(partial_q, "ctx").astype(jnp.bfloat16)
    rows = dec_hidden.shape[0]
    heads_dec = dec_q.shape[1] // HD
    kv_dec = seq_idx * heads_dec // group_size
    source = ctx_idx % n_seq
    mine = jnp.where(ctx_idx >= n_seq, jnp.stack([k_new, v_new]), jnp.stack([k_prefix, v_prefix]))
    span = spread(mine, "seq", source)
    span_k = head_cols(span[0], kv_dec)
    span_v = head_cols(span[1], kv_dec)
    dq_rows = dec_q.reshape(rows * heads_dec, HD)
    cache_pos = ctx_idx * block + jnp.arange(block, dtype=jnp.int32)
    length_rows = jnp.repeat(valid_len, heads_dec)
    parent_rows = jnp.repeat(parent, heads_dec)
    visible = jnp.where(
        cache_pos[None, :] < prefix_len,
        cache_pos[None, :] < length_rows[:, None],
        cache_pos[None, :] - prefix_len <= parent_rows[:, None],
    )
    start_state = (
        jnp.full((rows * heads_dec,), NEG_FILL, jnp.float32),
        jnp.zeros((rows * heads_dec,), jnp.float32),
        jnp.zeros((rows * heads_dec, HD), jnp.float32),
    )
    local = online_update(start_state, dq_rows, span_k, span_v, visible, scale)
    best, total, accum = joined(local, "ctx", combine_parts)
    own_keys = jnp.broadcast_to(
        head_cols(k_own, kv_dec)[:, None, :], (rows, heads_dec, HD)
    ).reshape(rows * heads_dec, HD)
    own_vals = jnp.broadcast_to(
        head_cols(v_own, kv_dec)[:, None, :], (rows, heads_dec, HD)
    ).reshape(rows * heads_dec, HD)
    own_score = jnp.sum(dq_rows.astype(jnp.float32) * own_keys.astype(jnp.float32), axis=1) * scale
    top = jnp.maximum(best, own_score)
    factor = jnp.exp(best - top)
    own_w = jnp.exp(own_score - top)
    own_r = lax.optimization_barrier(own_w.astype(jnp.bfloat16)).astype(jnp.float32)
    total = total * factor + own_w
    accum = accum * factor[:, None] + own_r[:, None] * own_vals.astype(jnp.float32)
    attn = (accum / total[:, None]).astype(jnp.bfloat16).reshape(rows, heads_dec * HD)
    out_weight = w_out.reshape(-1, w_out.shape[2])
    decoded = lax.psum_scatter(
        jnp.dot(attn, out_weight, preferred_element_type=jnp.float32).astype(jnp.bfloat16),
        ("seq", "head"),
        scatter_dimension=0,
        tiled=True,
    )
    return (prefill_out, decoded)


def solution(mesh):
    in_specs = (
        P("seq", ("head", "ctx")),
        P("seq", "head"),
        P("seq", "head"),
        P("seq", "head"),
        P("seq", "head"),
        P("seq"),
        P(None, "ctx"),
        P("ctx", "head", "seq"),
        P("head", "seq", "ctx"),
        P(None, "head"),
        P(None, "head"),
        P(),
        P(),
    )
    out_specs = (P("seq", ("head", "ctx")), P(("seq", "head"), "ctx"))
    return jax.shard_map(body, mesh=mesh, in_specs=in_specs, out_specs=out_specs, check_vma=False)
```

profile of v0, /device:TPU:0, one launch (start us, length us, event | category | flops | bytes accessed | tf_op | source)
XLA Modules:
  0.0 202.9 jit_solution(2038497784993934008)
XLA Ops:
  7.2 0.0 copy-start
  7.2 0.0 all-reduce.3.cloned.1.call-start
  7.2 2.2 %fusion.71 = bf16[2,512,256]{2,1,0:T(8,128)(2,1)} fusion(bf16[1,512,256]{2,1,0:T(8,128)(2,1)} %bitcast.135, bf16[1,512,256]{2,1,0:T(8,128)(2,1)} %bitcast.133, bf16[1,512,256]{2,1,0:T(8,128)(2,1)} %bitcast.134, bf16[1,512,256]{2,1,0:T(8,128)(2,1)} %bitcast.132, pred[]{:T(512)S(6)} %ge.18, pred[]{:T(512)S(6)} %eq.5), kind=kLoop, calls=%fused_computation.95 | loop fusion | flops 1048576 | bytes 1572866 | tf_op jit(solution)/shard_map/jit(_where)/select_n | solution.py:19
  9.4 0.0 all-reduce.3.cloned.1.call-update
  9.4 0.0 copy-start.14
  9.4 0.0 copy-start.15
  9.4 0.0 all-gather.5.cloned.1.call-start
  9.5 3.4 %fusion.55 = f32[256,1024]{1,0:T(8,128)S(1)} fusion(bf16[256,2048]{1,0:T(8,128)(2,1)S(1)} %copy-done, bf16[2048,1,1024]{2,0,1:T(8,128)(2,1)} %param.24), kind=kOutput, calls=%fused_computation.74 | convolution fusion | flops 1073741824 | bytes 6291456 | tf_op jit(solution)/shard_map/dot_general | solution.py:130
  12.9 45.1 %all-reduce.4 = bf16[256,1024]{1,0:T(8,128)(2,1)S(1)} all-reduce(f32[256,1024]{1,0:T(8,128)S(1)} %fusion.55), channel_id=1, replica_groups=mesh['seq'=2,'head'=4,'ctx'=4] {'ctx'}, use_global_device_ids=true, to_apply=%region_6.7 | all-reduce | flops 262144 | bytes 1572864 | tf_op jit(solution)/shard_map/psum | solution.py:133
  58.1 0.1 broadcast_in_dim.72
  58.2 0.1 le.20
  58.3 0.1 broadcast_in_dim.71
  58.4 0.1 lt.71
  58.5 0.2 reshape.115
  58.8 0.0 all-reduce.3.cloned.1.call-done
  58.8 1.1 fusion.88
  59.9 1.5 fusion.57
  61.4 2.2 %fusion.62 = f32[2048]{0:T(1024)S(1)} fusion(f32[2048,512]{0,1:T(8,128)S(1)} %get-tuple-element.353, f32[2048]{0:T(1024)S(1)} %broadcast_maximum_fusion, s32[2048]{0:T(1024)S(1)} %le.20, s32[2048]{0:T(1024)S(1)} %lt.71, s32[512]{0:T(512)S(1)} %fusion.82, s32[512]{0:T(512)S(1)} %iota_add_fusion.1, pred[512]{0:T(512)(128)(4,1)S(1)} %fusion.83), kind=kLoop, calls=%fused_computation.83 | loop fusion | flops 8386560 | bytes 4231680 | tf_op jit(solution)/shard_map/reduce_sum | solution.py:40
  63.6 0.0 copy-start.6
  63.6 0.0 copy-start.2
  63.6 0.0 copy-start.3
  63.6 0.0 copy-start.4
  63.6 3.3 %convolution_add_fusion.2 = f32[2048,128]{1,0:T(8,128)} fusion(f32[2048,512]{0,1:T(8,128)S(1)} %get-tuple-element.353, f32[2048]{0:T(1024)S(1)} %broadcast_maximum_fusion, s32[2048]{0:T(1024)S(1)} %le.20, s32[2048]{0:T(1024)S(1)} %lt.71, s32[512]{0:T(512)S(1)} %fusion.82, s32[512]{0:T(512)S(1)} %iota_add_fusion.1, pred[512]{0:T(512)(128)(4,1)S(1)} %fusion.83, ...), kind=kOutput, calls=%fused_computation.81 | convolution fusion | flops 277086208 | bytes 5411332 | tf_op jit(solution)/shard_map/dot_general | solution.py:41
  66.9 0.0 all-gather.5.cloned.1.call-update
  67.0 0.0 reduce-scatter.2.cloned.1.call-start
  67.1 1.1 reshape.109
  68.2 6.6 %all_gather.26 = bf16[1024,128]{1,0:T(8,128)(2,1)S(1)} all-gather(bf16[512,128]{1,0:T(8,128)(2,1)S(1)} %constant_dynamic-slice_fusion.5), channel_id=1, replica_groups=mesh['seq'=2,'head'=4,'ctx'=4] {'seq'}, dimensions={0}, use_global_device_ids=true | all-gather | bytes 393216 | tf_op jit(solution)/shard_map/all_gather | solution.py:101
  74.8 6.0 %all_gather.27 = bf16[1024,128]{1,0:T(8,128)(2,1)} all-gather(bf16[512,128]{1,0:T(8,128)(2,1)S(1)} %constant_dynamic-slice_fusion.4), channel_id=1, replica_groups=mesh['seq'=2,'head'=4,'ctx'=4] {'seq'}, dimensions={0}, use_global_device_ids=true | all-gather | bytes 393216 | tf_op jit(solution)/shard_map/all_gather | solution.py:103
  80.8 5.8 %all_gather.28 = bf16[1024,128]{1,0:T(8,128)(2,1)} all-gather(bf16[512,128]{1,0:T(8,128)(2,1)S(1)} %constant_dynamic-slice_fusion.3), channel_id=1, replica_groups=mesh['seq'=2,'head'=4,'ctx'=4] {'seq'}, dimensions={0}, use_global_device_ids=true | all-gather | bytes 393216 | tf_op jit(solution)/shard_map/all_gather | solution.py:102
  86.6 5.8 %all_gather.29 = bf16[1024,128]{1,0:T(8,128)(2,1)} all-gather(bf16[512,128]{1,0:T(8,128)(2,1)S(1)} %constant_dynamic-slice_fusion.2), channel_id=1, replica_groups=mesh['seq'=2,'head'=4,'ctx'=4] {'seq'}, dimensions={0}, use_global_device_ids=true | all-gather | bytes 393216 | tf_op jit(solution)/shard_map/all_gather | solution.py:104
  92.4 0.3 fusion.70
  92.8 13.3 %all-gather = f32[8192]{0:T(1024)S(1)} all-gather(f32[2048]{0:T(1024)S(1)} %broadcast_maximum_fusion), channel_id=2, replica_groups=mesh['seq'=2,'head'=4,'ctx'=4] {'ctx'}, dimensions={0}, use_global_device_ids=true | all-gather | bytes 40960 | tf_op jit(solution)/shard_map/all_gather | solution.py:23
  106.0 13.7 %all-gather.2 = f32[4,1,2048]{2,1,0:T(1,128)S(1)} all-gather(f32[1,1,2048]{2,1,0:T(1,128)S(1)} %bitcast.145), channel_id=1, replica_groups=mesh['seq'=2,'head'=4,'ctx'=4] {'ctx'}, dimensions={0}, use_global_device_ids=true | all-gather | bytes 40960 | tf_op jit(solution)/shard_map/all_gather | solution.py:23
  119.7 28.2 %all-gather.5.cloned.1.call-done = f32[8192,128]{1,0:T(8,128)} async-done(((f32[2048,128]{1,0:T(8,128)}), f32[8192,128]{1,0:T(8,128)}) %all-gather.5.cloned.1.call-update) | async-done | bytes 4194320 | tf_op jit(solution)/shard_map/all_gather | solution.py:23
  147.9 1.3 slice.18
  149.2 6.5 %while.34 = (s32[]{:T(128)}, f32[2048]{0:T(1024)S(1)}, f32[2048]{0:T(1024)S(1)}, f32[2048,128]{1,0:T(8,128)S(1)}, f32[4,2048]{1,0:T(4,128)S(1)}, /*index=5*/f32[...) while((s32[]{:T(128)}, f32[2048]{0:T(1024)S(1)}, f32[2048]{0:T(1024)S(1)}, ...), condition=%wide.region_11.12_spmd, body=%wide.region_10.11_spmd.sunk | while | flops 798725 | bytes 3260567 | solution.py:28
  149.3 2.1 %fusion.107 = f32[2048,128]{1,0:T(8,128)S(1)} fusion(f32[4,2048,128]{2,1,0:T(8,128)} %get-tuple-element.566, s32[]{:T(128)S(6)} %select_n.184, f32[2048,128]{1,0:T(8,128)S(1)} %get-tuple-element.553, f32[2048]{0:T(1024)S(1)} %get-tuple-element.476, f32[2048]{0:T(1024)S(1)} %get-tuple-element.477), kind=kLoop, calls=%fused_computation.3.clone.1 | loop fusion | flops 786432 | bytes 3162116 | tf_op jit(solution)/shard_map/while/body/eval_jaxpr/add | solution.py:54
  151.5 2.1 %fusion.107 = f32[2048,128]{1,0:T(8,128)S(1)} fusion(f32[4,2048,128]{2,1,0:T(8,128)} %get-tuple-element.566, s32[]{:T(128)S(6)} %select_n.184, f32[2048,128]{1,0:T(8,128)S(1)} %get-tuple-element.553, f32[2048]{0:T(1024)S(1)} %get-tuple-element.476, f32[2048]{0:T(1024)S(1)} %get-tuple-element.477), kind=kLoop, calls=%fused_computation.3.clone.1 | loop fusion | flops 786432 | bytes 3162116 | tf_op jit(solution)/shard_map/while/body/eval_jaxpr/add | solution.py:54
  153.6 2.1 %fusion.107 = f32[2048,128]{1,0:T(8,128)S(1)} fusion(f32[4,2048,128]{2,1,0:T(8,128)} %get-tuple-element.566, s32[]{:T(128)S(6)} %select_n.184, f32[2048,128]{1,0:T(8,128)S(1)} %get-tuple-element.553, f32[2048]{0:T(1024)S(1)} %get-tuple-element.476, f32[2048]{0:T(1024)S(1)} %get-tuple-element.477), kind=kLoop, calls=%fused_computation.3.clone.1 | loop fusion | flops 786432 | bytes 3162116 | tf_op jit(solution)/shard_map/while/body/eval_jaxpr/add | solution.py:54
  155.7 1.0 fusion.69
  156.7 0.2 reshape.116
  157.0 0.0 copy-start.7
  157.0 4.5 %fusion.58 = bf16[256,2048]{1,0:T(8,128)(2,1)} fusion(bf16[256,1024]{1,0:T(8,128)(2,1)S(1)} %reshape.116, bf16[1,1024,2048]{2,1,0:T(8,128)(2,1)} %param.25), kind=kOutput, calls=%fused_computation.80 | convolution fusion | flops 1074266112 | bytes 5767168 | tf_op jit(solution)/shard_map/dot_general | solution.py:174
  161.5 0.0 reduce-scatter.2.cloned.1.call-update
  161.6 25.2 %while.35 = (s32[]{:T(128)}, f32[2048]{0:T(1024)S(1)}, f32[2048]{0:T(1024)S(1)}, f32[2048,128]{1,0:T(8,128)S(1)}, s32[2]{0:T(128)S(1)}, /*index=5*/bf16[2,512,12...) while((s32[]{:T(128)}, f32[2048]{0:T(1024)S(1)}, ...), condition=%wide.region_5.6_spmd.clone, body=%wide.region_0.5_spmd.clone.sunk | while | flops 1108640256 | bytes 51171644 | solution.py:117
  161.6 0.1 broadcast_bitcast_fusion.2
  161.7 0.6 dynamic_slice.156
  162.3 0.6 iota_add_fusion.3
  162.9 2.7 %fusion.114 = (f32[2048]{0:T(1024)S(1)}, f32[512,2048]{1,0:T(8,128)}) fusion(s32[2048]{0:T(1024)S(1)} %bitcast.141, s32[512]{0:T(512)S(1)} %iota_add_fusion.3, bf16[2048,128]{1,0:T(8,128)(2,1)S(1)} %get-tuple-element.532, bf16[2,512,128]{2,1,0:T(8,128)(2,1)S(1)} %get-tuple-element.531, s32[]{:T(128)S(6)} %copy.25), kind=kOutput, calls=%fused_computation.13.clone.1 | convolution fusion | flops 272627712 | bytes 4868100 | tf_op jit(solution)/shard_map/while/body/eval_jaxpr/qd,kd->qk/dot_general | solution.py:35
  165.6 4.1 %fusion.116 = (f32[2048]{0:T(1024)S(1)}, f32[2048]{0:T(1024)S(1)}, f32[512,2048]{1,0:T(8,128)S(1)}) fusion(f32[512,2048]{1,0:T(8,128)} %get-tuple-element.491, f32[2048]{0:T(1024)S(1)} %select_maximum_fusion.2, s32[2048]{0:T(1024)S(1)} %bitcast.142, s32[512]{0:T(512)S(1)} %iota_add_fusion.3, s32[2048]{0:T(1024)S(1)} %fusion.115, ...), kind=kOutput, calls=%fused_computation.19.clone.1 | convolution fusion | flops 278917120 | bytes 9086980 | tf_op jit(solution)/shard_map/while/body/eval_jaxpr/qd,kd->qk/dot_general | solution.py:35
  169.8 1.2 fusion.117
  171.0 1.7 fusion.119
  172.8 1.4 convolution_add_fusion.4
  174.2 0.1 broadcast_bitcast_fusion.2
  174.3 0.6 dynamic_slice.156
  174.9 0.6 iota_add_fusion.3
  175.5 2.7 %fusion.114 = (f32[2048]{0:T(1024)S(1)}, f32[512,2048]{1,0:T(8,128)}) fusion(s32[2048]{0:T(1024)S(1)} %bitcast.141, s32[512]{0:T(512)S(1)} %iota_add_fusion.3, bf16[2048,128]{1,0:T(8,128)(2,1)S(1)} %get-tuple-element.532, bf16[2,512,128]{2,1,0:T(8,128)(2,1)S(1)} %get-tuple-element.531, s32[]{:T(128)S(6)} %copy.25), kind=kOutput, calls=%fused_computation.13.clone.1 | convolution fusion | flops 272627712 | bytes 4868100 | tf_op jit(solution)/shard_map/while/body/eval_jaxpr/qd,kd->qk/dot_general | solution.py:35
  178.2 4.1 %fusion.116 = (f32[2048]{0:T(1024)S(1)}, f32[2048]{0:T(1024)S(1)}, f32[512,2048]{1,0:T(8,128)S(1)}) fusion(f32[512,2048]{1,0:T(8,128)} %get-tuple-element.491, f32[2048]{0:T(1024)S(1)} %select_maximum_fusion.2, s32[2048]{0:T(1024)S(1)} %bitcast.142, s32[512]{0:T(512)S(1)} %iota_add_fusion.3, s32[2048]{0:T(1024)S(1)} %fusion.115, ...), kind=kOutput, calls=%fused_computation.19.clone.1 | convolution fusion | flops 278917120 | bytes 9086980 | tf_op jit(solution)/shard_map/while/body/eval_jaxpr/qd,kd->qk/dot_general | solution.py:35
  182.4 1.2 fusion.117
  183.6 1.7 fusion.119
  185.4 1.4 convolution_add_fusion.4
  186.8 0.3 divide_convert_fusion
  187.2 1.1 reshape.113
  188.3 8.1 %reduce-scatter.2.cloned.1.call-done = bf16[32,2048]{1,0:T(8,128)(2,1)} async-done(((bf16[256,2048]{1,0:T(8,128)(2,1)}), bf16[32,2048]{1,0:T(8,128)(2,1)}) %reduce-scatter.2.cloned.1.call-update) | async-done | bytes 131088 | tf_op jit(solution)/shard_map/reduce_scatter | solution.py:173
  (73 shorter events, 0.4 us)
Async XLA Ops:
  7.2 2.3 %copy-start = (bf16[256,2048]{1,0:T(8,128)(2,1)S(1)}, bf16[256,2048]{1,0:T(8,128)(2,1)}, u32[]{:S(2)}) copy-start(bf16[256,2048]{1,0:T(8,128)(2,1)} %param.23) | copy-start | bytes 3145732
  7.2 51.7 %all-reduce.3.cloned.1.call-start = ((), (), s32[]{:S(2)}) async-start(), calls=%async_computation.1 | async-start | bytes 1048576 | tf_op jit(solution)/shard_map/psum | solution.py:19
  9.4 48.7 %copy-start.14 = (s32[256]{0:T(256)S(1)}, s32[256]{0:T(256)}, u32[]{:S(2)}) copy-start(s32[256]{0:T(256)} %param.29) | copy-start | bytes 3076
  9.4 48.9 %copy-start.15 = (s32[256]{0:T(256)S(1)}, s32[256]{0:T(256)}, u32[]{:S(2)}) copy-start(s32[256]{0:T(256)} %param.28) | copy-start | bytes 3076
  9.4 138.5 %all-gather.5.cloned.1.call-start = ((), (), s32[]{:S(2)}) async-start(), calls=%async_computation.3 | async-start | bytes 5242880 | tf_op jit(solution)/shard_map/all_gather | solution.py:23
  63.6 3.5 %copy-start.6 = (bf16[512,512]{1,0:T(8,128)(2,1)S(1)}, bf16[512,512]{1,0:T(8,128)(2,1)}, u32[]{:S(2)}) copy-start(bf16[512,512]{1,0:T(8,128)(2,1)} %param.17) | copy-start | bytes 1572868
  63.6 4.6 %copy-start.2 = (bf16[512,256]{1,0:T(8,128)(2,1)S(1)}, bf16[512,256]{1,0:T(8,128)(2,1)}, u32[]{:S(2)}) copy-start(bf16[512,256]{1,0:T(8,128)(2,1)} %param.18) | copy-start | bytes 786436
  63.6 11.2 %copy-start.3 = (bf16[512,256]{1,0:T(8,128)(2,1)S(1)}, bf16[512,256]{1,0:T(8,128)(2,1)}, u32[]{:S(2)}) copy-start(bf16[512,256]{1,0:T(8,128)(2,1)} %param.20) | copy-start | bytes 786436
  63.6 17.2 %copy-start.4 = (bf16[512,256]{1,0:T(8,128)(2,1)S(1)}, bf16[512,256]{1,0:T(8,128)(2,1)}, u32[]{:S(2)}) copy-start(bf16[512,256]{1,0:T(8,128)(2,1)} %param.19) | copy-start | bytes 786436
  66.9 19.6 %copy-start.5 = (bf16[512,256]{1,0:T(8,128)(2,1)S(1)}, bf16[512,256]{1,0:T(8,128)(2,1)}, u32[]{:S(2)}) copy-start(bf16[512,256]{1,0:T(8,128)(2,1)} %param.21) | copy-start | bytes 786436
  66.9 25.4 %copy-start.11 = (bf16[256,256]{1,0:T(8,128)(2,1)S(1)}, bf16[256,256]{1,0:T(8,128)(2,1)}, u32[]{:S(2)}) copy-start(bf16[256,256]{1,0:T(8,128)(2,1)} %param.26) | copy-start | bytes 393220
  66.9 25.4 %copy-start.12 = (bf16[256,256]{1,0:T(8,128)(2,1)S(1)}, bf16[256,256]{1,0:T(8,128)(2,1)}, u32[]{:S(2)}) copy-start(bf16[256,256]{1,0:T(8,128)(2,1)} %param.27) | copy-start | bytes 393220
  67.0 129.4 %reduce-scatter.2.cloned.1.call-start = ((), (), s32[]{:S(2)}) async-start(), calls=%async_computation.2 | async-start | bytes 1179648 | tf_op jit(solution)/shard_map/reduce_scatter | solution.py:173
  157.0 4.6 %copy-start.1 = (f32[2048,128]{1,0:T(8,128)S(1)}, f32[2048,128]{1,0:T(8,128)}, u32[]{:S(2)}) copy-start(f32[2048,128]{1,0:T(8,128)} %custom-call.2) | copy-start | bytes 3145732
  157.0 4.6 %copy-start.7 = (bf16[2048,128]{1,0:T(8,128)(2,1)S(1)}, bf16[2048,128]{1,0:T(8,128)(2,1)}, u32[]{:S(2)}) copy-start(bf16[2048,128]{1,0:T(8,128)(2,1)} %reshape.109) | copy-start | bytes 1572868
  157.0 4.6 %copy-start.13 = (s32[4]{0:T(128)S(1)}, s32[4]{0:T(128)}, u32[]{:S(2)}) copy-start(s32[4]{0:T(128)} %param.22) | copy-start | bytes 52
  161.6 4.0 %copy-start.8 = (bf16[2,512,128]{2,1,0:T(8,128)(2,1)S(1)}, bf16[2,512,128]{2,1,0:T(8,128)(2,1)}, u32[]{:S(2)}) copy-start(bf16[2,512,128]{2,1,0:T(8,128)(2,1)} %get-tuple-element.533) | copy-start | bytes 786436 | tf_op jit(solution)/shard_map/while
  165.6 5.4 %copy-start.16 = (f32[512,2048]{1,0:T(8,128)S(1)}, f32[512,2048]{1,0:T(8,128)}, u32[]{:S(2)}) copy-start(f32[512,2048]{1,0:T(8,128)} %get-tuple-element.491) | copy-start | bytes 12582916 | tf_op jit(solution)/shard_map/while
  169.7 1.3 copy-start.9
  171.0 1.8 copy-start.10
  174.2 4.0 %copy-start.8 = (bf16[2,512,128]{2,1,0:T(8,128)(2,1)S(1)}, bf16[2,512,128]{2,1,0:T(8,128)(2,1)}, u32[]{:S(2)}) copy-start(bf16[2,512,128]{2,1,0:T(8,128)(2,1)} %get-tuple-element.533) | copy-start | bytes 786436 | tf_op jit(solution)/shard_map/while
  178.2 5.4 %copy-start.16 = (f32[512,2048]{1,0:T(8,128)S(1)}, f32[512,2048]{1,0:T(8,128)}, u32[]{:S(2)}) copy-start(f32[512,2048]{1,0:T(8,128)} %get-tuple-element.491) | copy-start | bytes 12582916 | tf_op jit(solution)/shard_map/while
  182.3 1.3 copy-start.9
  183.6 1.8 copy-start.10
Sparse Core Ops, SparseCore 0:
  10.9 31.2 all-reduce.2
  67.1 80.7 all-gather.4
  161.7 34.6 reduce-scatter.1
where the time goes:
time: 203 us
  blocking collectives  96.1 us (47%)
  waiting for transfers between devices  36.4 us (18%)
  matrix products  32.6 us (16%)
  other arithmetic  16.1 us (8%)
  between operations  14.2 us (7%)
  local copies, waits for them, and re-layouts  6.98 us (3%)
    psum x1, blocking collectives, body(): dec_q = lax.psum(partial_q, 'ctx').astype(jnp.bfloat16)  45.1 us
    all_gather x1, waiting for transfers between devices, joined(): gathered = jax.tree.map(lambda a: lax.all_gather(a, axis), part)  28.2 us
    all_gather x2, blocking collectives, joined(): gathered = jax.tree.map(lambda a: lax.all_gather(a, axis), part)  26.9 us
    dot_general x5, matrix products, online_update(): jnp.einsum('qd,kd->qk', queries, keys, preferred_element_type=jnp.float32)  15 us
    dot_general x5, matrix products, online_update(): jnp.dot(weights.astype(jnp.bfloat16), values, preferred_element_type=jnp....  9.59 us
    reduce_scatter x1, waiting for transfers between devices, body(): lax.psum_scatter(jnp.dot(attn, out_weight, preferred_element_type=jnp.flo...  8.09 us
    all_gather x1, blocking collectives, body(): kp = lax.all_gather(spans[0], 'seq', axis=0, tiled=True)  6.63 us
    add x3, other arithmetic, combine_parts(): left[2] * left_f[:, None] + right[2] * right_f[:, None]  6.26 us
  transfers between devices with their start and end apart: 3, of which 2 were waited for; matrix products, arithmetic and copies ran while one was open for 16% of the time, Pallas kernels for 0%

commit v1 on v0

v1 whole, which is shorter than its diff:
```python
import functools
import math

import jax
import jax.numpy as jnp
from jax import lax
from jax.experimental import pallas as pl
from jax.experimental.pallas import tpu as pltpu
from jax.sharding import PartitionSpec as P

HQ = 64
KVH = 8
HD = 128
QBLK = 128
GROUP = HQ // KVH
NEG = -1e30
MESH = pl.DeviceIdType.MESH
F32 = jnp.float32
BF16 = jnp.bfloat16
C2 = math.log2(math.e) / math.sqrt(HD)


def dot_t(a, b):
    return lax.dot_general(a, b, (((1,), (1,)), ((), ())), preferred_element_type=F32)


def absorb(state, queries, keys, values, visible):
    best, total, accum = state
    scores = jnp.where(visible, dot_t(queries, keys) * C2, NEG)
    fresh = jnp.maximum(best, jnp.max(scores, axis=1, keepdims=True))
    factor = jnp.exp2(best - fresh)
    weights = jnp.exp2(scores - fresh)
    total = total * factor + jnp.sum(weights, axis=1, keepdims=True)
    accum = accum * factor + jnp.dot(weights.astype(BF16), values, preferred_element_type=F32)
    return fresh, total, accum


def kernel(
    sizes,
    q_hbm, kp_hbm, vp_hbm, kn_hbm, vn_hbm, off_ref, x_hbm, wq_hbm, wo_hbm, ko_ref, vo_ref, lim_ref,
    pre_ref, dec_ref,
    q, kv, x, wq, wo, qpart, qrecv, attn, opart, orecv, m_s, l_s, a_s,
    load_sem, wq_sem, wo_sem, kv_load, kv_send, kv_recv, q_send, q_recv, a_send, a_recv, o_send, o_recv,
):
    n_seq, n_head, n_ctx, q_chunk, o_chunk = sizes
    seq, head, ctx = lax.axis_index("seq"), lax.axis_index("head"), lax.axis_index("ctx")
    block, width = q.shape
    per_dev = width // HD
    n_blk = block // QBLK
    n_out = n_seq * n_head
    me_out = seq * n_head + head
    rows, cols_q = x.shape[0], wq.shape[1]
    r_ctx, r_out = rows // n_ctx, rows // n_out
    heads_dec = cols_q // HD
    n_qc, n_oc = cols_q // q_chunk, wo.shape[1] // o_chunk

    load_x = pltpu.make_async_copy(x_hbm, x, load_sem.at[0])
    load_x.start()
    load_wq = []
    for c in range(n_qc):
        part = pl.ds(c * q_chunk, q_chunk)
        load_wq.append(pltpu.make_async_copy(wq_hbm.at[:, part], wq.at[:, part], wq_sem.at[c]))
        load_wq[-1].start()
    sources = (kp_hbm, vp_hbm, kn_hbm, vn_hbm)
    load_kv = [pltpu.make_async_copy(s, kv.at[0, i], kv_load.at[i]) for i, s in enumerate(sources)]
    load_q = pltpu.make_async_copy(q_hbm, q, load_sem.at[1])
    for c in load_kv + [load_q]:
        c.start()
    load_wo = pltpu.make_async_copy(wo_hbm, wo, wo_sem)
    load_wo.start()

    def out_peer(d):
        t = lax.rem(me_out + d, n_out)
        return {"seq": t // n_head, "head": lax.rem(t, n_head)}

    barrier = pltpu.get_barrier_semaphore()
    for d in range(1, n_ctx):
        pl.semaphore_signal(
            barrier, inc=1, device_id={"ctx": lax.rem(ctx + d, n_ctx)}, device_id_type=MESH
        )
    for d in range(1, n_out):
        pl.semaphore_signal(barrier, inc=1, device_id=out_peer(d), device_id_type=MESH)
    pl.semaphore_wait(barrier, n_ctx - 1 + n_out - 1)

    def remote(src, dst, send, recv, to):
        copy = pltpu.make_async_remote_copy(
            src_ref=src, dst_ref=dst, send_sem=send, recv_sem=recv, device_id=to, device_id_type=MESH
        )
        copy.start()
        return copy

    sent = []
    kv_copies = []
    for d in range(1, n_seq):
        to = {"seq": lax.rem(seq + d, n_seq)}
        for i, s in enumerate(sources):
            kv_copies.append(remote(s, kv.at[d, i], kv_send.at[d, i], kv_recv.at[d, i], to))

    load_x.wait()
    q_copies = []
    for c in range(n_qc):
        load_wq[c].wait()
        part = slice(c * q_chunk, (c + 1) * q_chunk)
        prod = jnp.dot(x[...], wq[:, part], preferred_element_type=F32)
        for i in range(n_ctx):
            qpart[c, i] = prod[i * r_ctx:(i + 1) * r_ctx]
        for d in range(1, n_ctx):
            to = lax.rem(ctx + d, n_ctx)
            q_copies.append(
                remote(qpart.at[c, to], qrecv.at[c, d], q_send.at[c, d], q_recv.at[c, d], {"ctx": to})
            )

    def stacked(b):
        tokens = pl.ds(pl.multiple_of(b * QBLK, QBLK), QBLK)
        return jnp.concatenate([q[tokens, h * HD:(h + 1) * HD] for h in range(per_dev)], axis=0)

    lanes_pre = pl.ds(pl.multiple_of(ctx * per_dev // GROUP * HD, HD), HD)
    token = lax.broadcasted_iota(jnp.int32, (QBLK, block), 0)
    key = lax.broadcasted_iota(jnp.int32, (QBLK, block), 1)

    def tile(a, n):
        return jnp.concatenate([a] * n, axis=0) if n > 1 else a

    def prefill_step(state, queries, b, d):
        base = lax.rem(seq - d + n_seq, n_seq) * block
        seen = key + base <= token + (seq * block + b * QBLK)
        state = absorb(
            state, queries, kv[d, 2, :, lanes_pre], kv[d, 3, :, lanes_pre], tile(seen, per_dev)
        )
        seen = key + base >= off_ref[b]
        return absorb(
            state, queries, kv[d, 0, :, lanes_pre], kv[d, 1, :, lanes_pre], tile(seen, per_dev)
        )

    for c in load_kv + [load_q]:
        c.wait()
    rp = per_dev * QBLK

    def local_block(b, _):
        zero = jnp.zeros((rp, 1), F32)
        m, l, a = prefill_step((zero + NEG, zero, jnp.zeros((rp, HD), F32)), stacked(b), b, 0)
        m_s[b], l_s[b], a_s[b] = m, l, a
        return 0

    lax.fori_loop(0, n_blk, local_block, 0)

    for c in kv_copies:
        c.wait_recv()
    for c in q_copies:
        c.wait_recv()
    parts = []
    for c in range(n_qc):
        total = qpart[c, ctx]
        for d in range(1, n_ctx):
            total = total + qrecv[c, d]
        total = total.astype(BF16)
        parts += [total[:, h * HD:(h + 1) * HD] for h in range(q_chunk // HD)]
    dq = jnp.concatenate(parts, axis=0)
    lanes_dec = pl.ds(pl.multiple_of(seq * heads_dec // GROUP * HD, HD), HD)
    mine = pl.ds(pl.multiple_of(ctx * r_ctx, r_ctx), r_ctx)
    own_k = tile(ko_ref[mine, lanes_dec].astype(F32), heads_dec)
    own_v = tile(vo_ref[mine, lanes_dec].astype(F32), heads_dec)
    limits = lim_ref[mine, :]
    length, parent = limits[:, 0:1], limits[:, 1:2]
    own = jnp.sum(dq.astype(F32) * own_k, axis=1, keepdims=True) * C2
    dkey = lax.broadcasted_iota(jnp.int32, (r_ctx, block), 1)

    def decode_step(d, state):
        pos = dkey + lax.rem(seq - d + n_seq, n_seq) * block
        state = absorb(
            state, dq, kv[d, 0, :, lanes_dec], kv[d, 1, :, lanes_dec], tile(pos < length, heads_dec)
        )
        return absorb(
            state, dq, kv[d, 2, :, lanes_dec], kv[d, 3, :, lanes_dec], tile(pos <= parent, heads_dec)
        )

    _, total, accum = lax.fori_loop(0, n_seq, decode_step, (own, jnp.ones_like(own), own_v))
    result = (accum / total).astype(BF16)
    for h in range(heads_dec):
        attn[0, :, h * HD:(h + 1) * HD] = result[h * r_ctx:(h + 1) * r_ctx]
    a_copies = [
        remote(attn.at[0], attn.at[d], a_send.at[d], a_recv.at[d], {"ctx": lax.rem(ctx + d, n_ctx)})
        for d in range(1, n_ctx)
    ]

    def remote_block(b, _):
        queries = stacked(b)
        state = lax.fori_loop(
            1, n_seq, lambda d, st: prefill_step(st, queries, b, d), (m_s[b], l_s[b], a_s[b])
        )
        out = (state[2] / state[1]).astype(BF16)
        tokens = pl.ds(pl.multiple_of(b * QBLK, QBLK), QBLK)
        for h in range(per_dev):
            pre_ref[tokens, h * HD:(h + 1) * HD] = out[h * QBLK:(h + 1) * QBLK]
        return 0

    lax.fori_loop(0, n_blk, remote_block, 0)

    load_wo.wait()
    for c in a_copies:
        c.wait_recv()
    full = jnp.concatenate([attn[lax.rem(ctx - i + n_ctx, n_ctx)] for i in range(n_ctx)], axis=0)
    o_copies = []
    for c in range(n_oc):
        prod = jnp.dot(full, wo[:, c * o_chunk:(c + 1) * o_chunk], preferred_element_type=F32)
        for i in range(n_out):
            opart[c, i] = prod[i * r_out:(i + 1) * r_out].astype(BF16)
        for d in range(1, n_out):
            to = lax.rem(me_out + d, n_out)
            o_copies.append(
                remote(opart.at[c, to], orecv.at[c, d], o_send.at[c, d], o_recv.at[c, d], out_peer(d))
            )
    for c in range(n_oc):
        acc = opart[c, me_out].astype(F32)
        for d in range(1, n_out):
            o_copies[c * (n_out - 1) + d - 1].wait_recv()
            acc = acc + orecv[c, d].astype(F32)
        dec_ref[:, c * o_chunk:(c + 1) * o_chunk] = acc.astype(BF16)
    for c in kv_copies + q_copies + a_copies + o_copies:
        c.wait_send()


def body(
    q_new, k_prefix, v_prefix, k_new, v_new, block_offsets, dec_hidden, w_query, w_out, k_own, v_own,
    valid_len, parent,
):
    n_seq, n_head, n_ctx = (lax.axis_size(a) for a in ("seq", "head", "ctx"))
    n_out = n_seq * n_head
    block, width = q_new.shape
    rows = dec_hidden.shape[0]
    wq = w_query.reshape(w_query.shape[0], -1)
    wo = w_out.reshape(-1, w_out.shape[2])
    q_chunk = math.gcd(wq.shape[1], 512)
    o_chunk = math.gcd(wo.shape[1], 512)
    n_qc, n_oc = wq.shape[1] // q_chunk, wo.shape[1] // o_chunk
    limits = jnp.stack([valid_len, parent], axis=1)
    n_blk, rp = block // QBLK, width // HD * QBLK
    hbm, vmem = pl.BlockSpec(memory_space=pl.ANY), pl.BlockSpec(memory_space=pltpu.VMEM)
    smem = pl.BlockSpec(memory_space=pltpu.SMEM)
    dma = pltpu.SemaphoreType.DMA
    r_ctx, r_out = rows // n_ctx, rows // n_out
    return pl.pallas_call(
        functools.partial(kernel, (n_seq, n_head, n_ctx, q_chunk, o_chunk)),
        out_shape=(
            jax.ShapeDtypeStruct(q_new.shape, BF16),
            jax.ShapeDtypeStruct((r_out, wo.shape[1]), BF16),
        ),
        in_specs=[hbm] * 5 + [smem] + [hbm] * 3 + [vmem] * 3,
        out_specs=(vmem, vmem),
        scratch_shapes=[
            pltpu.VMEM(q_new.shape, BF16),
            pltpu.VMEM((n_seq, 4) + k_new.shape, BF16),
            pltpu.VMEM(dec_hidden.shape, BF16),
            pltpu.VMEM(wq.shape, BF16),
            pltpu.VMEM(wo.shape, BF16),
            pltpu.VMEM((n_qc, n_ctx, r_ctx, q_chunk), F32),
            pltpu.VMEM((n_qc, n_ctx, r_ctx, q_chunk), F32),
            pltpu.VMEM((n_ctx, r_ctx, wo.shape[0]), BF16),
            pltpu.VMEM((n_oc, n_out, r_out, o_chunk), BF16),
            pltpu.VMEM((n_oc, n_out, r_out, o_chunk), BF16),
            pltpu.VMEM((n_blk, rp, 1), F32),
            pltpu.VMEM((n_blk, rp, 1), F32),
            pltpu.VMEM((n_blk, rp, HD), F32),
            dma((2,)), dma((n_qc,)), dma, dma((4,)),
            dma((n_seq, 4)), dma((n_seq, 4)),
            dma((n_qc, n_ctx)), dma((n_qc, n_ctx)),
            dma((n_ctx,)), dma((n_ctx,)),
            dma((n_oc, n_out)), dma((n_oc, n_out)),
        ],
        compiler_params=pltpu.CompilerParams(
            collective_id=0, has_side_effects=True, vmem_limit_bytes=56 * 1024 * 1024
        ),
    )(q_new, k_prefix, v_prefix, k_new, v_new, block_offsets, dec_hidden, wq, wo, k_own, v_own, limits)


def solution(mesh):
    in_specs = (
        P("seq", ("head", "ctx")),
        P("seq", "head"),
        P("seq", "head"),
        P("seq", "head"),
        P("seq", "head"),
        P("seq"),
        P(None, "ctx"),
        P("ctx", "head", "seq"),
        P("head", "seq", "ctx"),
        P(None, "head"),
        P(None, "head"),
        P(),
        P(),
    )
    out_specs = (P("seq", ("head", "ctx")), P(("seq", "head"), "ctx"))
    return jax.shard_map(body, mesh=mesh, in_specs=in_specs, out_specs=out_specs, check_vma=False)
```

time: 203 us -> 65.1 us (0.32)
  blocking collectives: 96.1 us -> 0 us
  Pallas kernels: 0 us -> 59.3 us
  waiting for transfers between devices: 36.4 us -> 0 us
  matrix products: 32.6 us -> 0 us
  other arithmetic: 16.1 us -> 0.7 us
  between operations: 14.2 us -> 0.64 us
  local copies, waits for them, and re-layouts: 6.98 us -> 4.24 us
    pallas_call x0 -> x1, Pallas kernels: none -> 59.3 us  [body(): pl.pallas_call(functools.partial(kernel, (n_seq, n_head, n_ctx, q_chunk,...]
    all_gather x6 -> x0, blocking collectives: 51 us -> none  [the longest x2 26.9 us: joined(): gathered = jax.tree.map(lambda a: lax.all_gather(a, axis), part)]
    psum x1 -> x0, blocking collectives: 45.1 us -> none  [body(): dec_q = lax.psum(partial_q, 'ctx').astype(jnp.bfloat16)]
    dot_general x12 -> x0, matrix products: 32.6 us -> none  [the longest x5 15 us: online_update(): jnp.einsum('qd,kd->qk', queries, keys, preferred_element_type=jnp.float32)]
    all_gather x1 -> x0, waiting for transfers between devices: 28.2 us -> none  [joined(): gathered = jax.tree.map(lambda a: lax.all_gather(a, axis), part)]
    reduce_scatter x1 -> x0, waiting for transfers between devices: 8.09 us -> none  [body(): lax.psum_scatter(jnp.dot(attn, out_weight, preferred_element_type=jnp.flo...]
    add x13 -> x0, other arithmetic: 7.65 us -> none  [the longest x3 6.26 us: combine_parts(): left[2] * left_f[:, None] + right[2] * right_f[:, None]]
    reduce_sum x4 -> x0, other arithmetic: 4.88 us -> none  [the longest x3 4.53 us: online_update(): total = total * factor + jnp.sum(weights, axis=1)]
  transfers between devices with their start and end apart: 3 -> 0, of which waited for: 2 -> 0; matrix products, arithmetic and copies ran while one was open for 16% -> 0% of each run, Pallas kernels for 0% -> 0%
where the time goes in v1:
time: 65.1 us; the launch traced here: 64.9 us
  Pallas kernels  59.3 us (91%)
  local copies, waits for them, and re-layouts  4.24 us (7%)
  other arithmetic  0.7 us (1%)
    pallas_call x1, Pallas kernels, body(): pl.pallas_call(functools.partial(kernel, (n_seq, n_head, n_ctx, q_chunk,...  59.3 us
    unnamed x2, local copies, waits for them, and re-layouts  3.44 us

profile of v1, /device:TPU:0, one launch (start us, length us, event | category | flops | bytes accessed | tf_op | source)
XLA Modules:
  0.0 64.9 jit_solution(1403776504946047866)
XLA Ops:
  0.6 0.7 %pad_add_fusion = s32[256,2]{0,1:T(2,128)S(1)} fusion(s32[256,1]{0,1:T(1,128)} %bitcast.6, s32[256,1]{0,1:T(1,128)} %bitcast.7), kind=kLoop, calls=%fused_computation | loop fusion | flops 512 | bytes 4096 | tf_op jit(solution)/shard_map/stack | solution.py:236
  1.3 0.8 %copy.17.lim_ref = s32[256,2]{1,0:T(8,128)} copy(s32[256,2]{0,1:T(2,128)S(1)} %pad_add_fusion) | data formatting | bytes 4096 | tf_op jit(solution)/shard_map/stack | solution.py:236
  2.1 59.3 %shard_map.140 = (bf16[512,512]{1,0:T(8,128)(2,1)}, bf16[32,2048]{1,0:T(8,128)(2,1)}) custom-call(bf16[512,512]{1,0:T(8,128)(2,1)} %q_hbm.1, bf16[512,256]{1,0:T(8,128)(2,1)} %kp_hbm.1, bf16[512,256]{1,0:T(8,128)(2,1)} %vp_hbm.1, bf16[512,256]{1,0:T(8,128)(2,1)} %kn_hbm.1, bf16[512,256]{1,0:T(8,128)(2,1)} %vn_hbm.1, s32[4]{0:T(128)} %off_ref.1, ...), custom_call_target="tpu_custom_call" | custom-call | tf_op jit(solution)/shard_map/pallas_call | solution.py:242
  61.4 1.9 %copy.20 = bf16[512,512]{1,0:T(8,128)(2,1)} copy(bf16[512,512]{1,0:T(8,128)(2,1)} %get-tuple-element.4) | data formatting | bytes 1048576
  63.3 1.6 %copy.21 = bf16[32,2048]{1,0:T(8,128)(2,1)} copy(bf16[32,2048]{1,0:T(8,128)(2,1)} %get-tuple-element.5) | data formatting | bytes 262144

commit v2 on v1

--- a/solution.py
+++ b/solution.py
@@ -37,16 +37,17 @@
 
 def kernel(
     sizes,
-    q_hbm, kp_hbm, vp_hbm, kn_hbm, vn_hbm, off_ref, x_hbm, wq_hbm, wo_hbm, ko_ref, vo_ref, lim_ref,
+    q_hbm, kp_hbm, vp_hbm, kn_hbm, vn_hbm, off_ref, x_hbm, wq_hbm, wo_hbm, ko_ref, vo_ref, len_ref, par_ref,
     pre_ref, dec_ref,
-    q, kv, x, wq, wo, qpart, qrecv, attn, opart, orecv, m_s, l_s, a_s,
-    load_sem, wq_sem, wo_sem, kv_load, kv_send, kv_recv, q_send, q_recv, a_send, a_recv, o_send, o_recv,
+    q, kv, x, wq, wo, qpart, qrecv, attn, opart, pair, osum, orecv, m_s, l_s, a_s,
+    load_sem, wq_sem, wo_sem, kv_load, kv_send, kv_recv, q_send, q_recv, a_send, a_recv, p_send, p_recv, o_send, o_recv,
 ):
     n_seq, n_head, n_ctx, q_chunk, o_chunk = sizes
     seq, head, ctx = lax.axis_index("seq"), lax.axis_index("head"), lax.axis_index("ctx")
     block, width = q.shape
     per_dev = width // HD
     n_blk = block // QBLK
+    n_kvh = kv.shape[3] // HD
     n_out = n_seq * n_head
     me_out = seq * n_head + head
     rows, cols_q = x.shape[0], wq.shape[1]
@@ -89,12 +90,19 @@
         copy.start()
         return copy
 
-    sent = []
-    kv_copies = []
+    kv_copies = [[] for _ in range(n_kvh)]
     for d in range(1, n_seq):
         to = {"seq": lax.rem(seq + d, n_seq)}
-        for i, s in enumerate(sources):
-            kv_copies.append(remote(s, kv.at[d, i], kv_send.at[d, i], kv_recv.at[d, i], to))
+        first = to["seq"] * heads_dec // GROUP
+        for j in range(n_kvh):
+            lanes = pl.ds(pl.multiple_of(lax.rem(first + j, n_kvh) * HD, HD), HD)
+            for i, s in enumerate(sources):
+                kv_copies[j].append(
+                    remote(
+                        s.at[:, lanes], kv.at[d, i, :, lanes],
+                        kv_send.at[d, i, j], kv_recv.at[d, i, j], to,
+                    )
+                )
 
     load_x.wait()
     q_copies = []
@@ -144,44 +152,51 @@
 
     lax.fori_loop(0, n_blk, local_block, 0)
 
-    for c in kv_copies:
+    lanes_dec = pl.ds(pl.multiple_of(seq * heads_dec // GROUP * HD, HD), HD)
+    mine = pl.ds(pl.multiple_of(ctx * r_ctx, r_ctx), r_ctx)
+    h_chunk = q_chunk // HD
+    own_k = tile(ko_ref[mine, lanes_dec].astype(F32), h_chunk)
+    own_v = tile(vo_ref[mine, lanes_dec].astype(F32), h_chunk)
+    row_at = lax.broadcasted_iota(jnp.int32, (r_ctx, rows), 0) + ctx * r_ctx
+    diagonal = row_at == lax.broadcasted_iota(jnp.int32, (r_ctx, rows), 1)
+    length = jnp.sum(jnp.where(diagonal, len_ref[...], 0), axis=1, keepdims=True)
+    parent = jnp.sum(jnp.where(diagonal, par_ref[...], 0), axis=1, keepdims=True)
+    dkey = lax.broadcasted_iota(jnp.int32, (r_ctx, block), 1)
+
+    def decode_step(d, state, dq):
+        pos = dkey + lax.rem(seq - d + n_seq, n_seq) * block
+        state = absorb(
+            state, dq, kv[d, 0, :, lanes_dec], kv[d, 1, :, lanes_dec], tile(pos < length, h_chunk)
+        )
+        return absorb(
+            state, dq, kv[d, 2, :, lanes_dec], kv[d, 3, :, lanes_dec], tile(pos <= parent, h_chunk)
+        )
+
+    for c in kv_copies[0]:
         c.wait_recv()
-    for c in q_copies:
-        c.wait_recv()
-    parts = []
+    a_copies = []
     for c in range(n_qc):
+        for d in range(1, n_ctx):
+            q_copies[c * (n_ctx - 1) + d - 1].wait_recv()
         total = qpart[c, ctx]
         for d in range(1, n_ctx):
             total = total + qrecv[c, d]
         total = total.astype(BF16)
-        parts += [total[:, h * HD:(h + 1) * HD] for h in range(q_chunk // HD)]
-    dq = jnp.concatenate(parts, axis=0)
-    lanes_dec = pl.ds(pl.multiple_of(seq * heads_dec // GROUP * HD, HD), HD)
-    mine = pl.ds(pl.multiple_of(ctx * r_ctx, r_ctx), r_ctx)
-    own_k = tile(ko_ref[mine, lanes_dec].astype(F32), heads_dec)
-    own_v = tile(vo_ref[mine, lanes_dec].astype(F32), heads_dec)
-    limits = lim_ref[mine, :]
-    length, parent = limits[:, 0:1], limits[:, 1:2]
-    own = jnp.sum(dq.astype(F32) * own_k, axis=1, keepdims=True) * C2
-    dkey = lax.broadcasted_iota(jnp.int32, (r_ctx, block), 1)
-
-    def decode_step(d, state):
-        pos = dkey + lax.rem(seq - d + n_seq, n_seq) * block
-        state = absorb(
-            state, dq, kv[d, 0, :, lanes_dec], kv[d, 1, :, lanes_dec], tile(pos < length, heads_dec)
-        )
-        return absorb(
-            state, dq, kv[d, 2, :, lanes_dec], kv[d, 3, :, lanes_dec], tile(pos <= parent, heads_dec)
-        )
-
-    _, total, accum = lax.fori_loop(0, n_seq, decode_step, (own, jnp.ones_like(own), own_v))
-    result = (accum / total).astype(BF16)
-    for h in range(heads_dec):
-        attn[0, :, h * HD:(h + 1) * HD] = result[h * r_ctx:(h + 1) * r_ctx]
-    a_copies = [
-        remote(attn.at[0], attn.at[d], a_send.at[d], a_recv.at[d], {"ctx": lax.rem(ctx + d, n_ctx)})
-        for d in range(1, n_ctx)
-    ]
+        dq = jnp.concatenate([total[:, h * HD:(h + 1) * HD] for h in range(h_chunk)], axis=0)
+        own = jnp.sum(dq.astype(F32) * own_k, axis=1, keepdims=True) * C2
+        _, total, accum = lax.fori_loop(
+            0, n_seq, lambda d, state: decode_step(d, state, dq), (own, jnp.ones_like(own), own_v)
+        )
+        result = (accum / total).astype(BF16)
+        for h in range(h_chunk):
+            attn[c, 0, :, h * HD:(h + 1) * HD] = result[h * r_ctx:(h + 1) * r_ctx]
+        for d in range(1, n_ctx):
+            a_copies.append(
+                remote(
+                    attn.at[c, 0], attn.at[c, d], a_send.at[c, d], a_recv.at[c, d],
+                    {"ctx": lax.rem(ctx + d, n_ctx)},
+                )
+            )
 
     def remote_block(b, _):
         queries = stacked(b)
@@ -194,29 +209,49 @@
             pre_ref[tokens, h * HD:(h + 1) * HD] = out[h * QBLK:(h + 1) * QBLK]
         return 0
 
-    lax.fori_loop(0, n_blk, remote_block, 0)
-
     load_wo.wait()
     for c in a_copies:
         c.wait_recv()
-    full = jnp.concatenate([attn[lax.rem(ctx - i + n_ctx, n_ctx)] for i in range(n_ctx)], axis=0)
-    o_copies = []
+    full = jnp.concatenate(
+        [
+            jnp.concatenate(
+                [attn[c, lax.rem(ctx - i + n_ctx, n_ctx)] for i in range(n_ctx)], axis=0
+            )
+            for c in range(n_qc)
+        ],
+        axis=1,
+    )
+    core = lax.rem(head, 2)
+    other = {"head": head + 1 - 2 * core}
+    p_copies, o_copies = [], []
     for c in range(n_oc):
         prod = jnp.dot(full, wo[:, c * o_chunk:(c + 1) * o_chunk], preferred_element_type=F32)
         for i in range(n_out):
-            opart[c, i] = prod[i * r_out:(i + 1) * r_out].astype(BF16)
-        for d in range(1, n_out):
-            to = lax.rem(me_out + d, n_out)
+            opart[c, i % 2, i // 2] = prod[i * r_out:(i + 1) * r_out].astype(BF16)
+        p_copies.append(
+            remote(opart.at[c, 1 - core], pair.at[c], p_send.at[c], p_recv.at[c], other)
+        )
+    for c in range(n_oc):
+        p_copies[c].wait_recv()
+        for i in range(n_out // 2):
+            osum[c, i] = (opart[c, core, i].astype(F32) + pair[c, i].astype(F32)).astype(BF16)
+        for d in range(1, n_out // 2):
+            t = lax.rem(me_out // 2 + d, n_out // 2)
+            to = {"seq": t // (n_head // 2), "head": lax.rem(t, n_head // 2) * 2 + core}
             o_copies.append(
-                remote(opart.at[c, to], orecv.at[c, d], o_send.at[c, d], o_recv.at[c, d], out_peer(d))
+                remote(osum.at[c, t], orecv.at[c, d], o_send.at[c, d], o_recv.at[c, d], to)
             )
+    for group in kv_copies[1:]:
+        for c in group:
+            c.wait_recv()
+    lax.fori_loop(0, n_blk, remote_block, 0)
     for c in range(n_oc):
-        acc = opart[c, me_out].astype(F32)
-        for d in range(1, n_out):
-            o_copies[c * (n_out - 1) + d - 1].wait_recv()
+        acc = osum[c, me_out // 2].astype(F32)
+        for d in range(1, n_out // 2):
+            o_copies[c * (n_out // 2 - 1) + d - 1].wait_recv()
             acc = acc + orecv[c, d].astype(F32)
         dec_ref[:, c * o_chunk:(c + 1) * o_chunk] = acc.astype(BF16)
-    for c in kv_copies + q_copies + a_copies + o_copies:
+    for c in sum(kv_copies, []) + q_copies + a_copies + p_copies + o_copies:
         c.wait_send()
 
 
@@ -233,7 +268,7 @@
     q_chunk = math.gcd(wq.shape[1], 512)
     o_chunk = math.gcd(wo.shape[1], 512)
     n_qc, n_oc = wq.shape[1] // q_chunk, wo.shape[1] // o_chunk
-    limits = jnp.stack([valid_len, parent], axis=1)
+    n_kvh = k_new.shape[1] // HD
     n_blk, rp = block // QBLK, width // HD * QBLK
     hbm, vmem = pl.BlockSpec(memory_space=pl.ANY), pl.BlockSpec(memory_space=pltpu.VMEM)
     smem = pl.BlockSpec(memory_space=pltpu.SMEM)
@@ -245,7 +280,7 @@
             jax.ShapeDtypeStruct(q_new.shape, BF16),
             jax.ShapeDtypeStruct((r_out, wo.shape[1]), BF16),
         ),
-        in_specs=[hbm] * 5 + [smem] + [hbm] * 3 + [vmem] * 3,
+        in_specs=[hbm] * 5 + [smem] + [hbm] * 3 + [vmem] * 4,
         out_specs=(vmem, vmem),
         scratch_shapes=[
             pltpu.VMEM(q_new.shape, BF16),
@@ -255,22 +290,25 @@
             pltpu.VMEM(wo.shape, BF16),
             pltpu.VMEM((n_qc, n_ctx, r_ctx, q_chunk), F32),
             pltpu.VMEM((n_qc, n_ctx, r_ctx, q_chunk), F32),
-            pltpu.VMEM((n_ctx, r_ctx, wo.shape[0]), BF16),
-            pltpu.VMEM((n_oc, n_out, r_out, o_chunk), BF16),
-            pltpu.VMEM((n_oc, n_out, r_out, o_chunk), BF16),
+            pltpu.VMEM((n_qc, n_ctx, r_ctx, q_chunk), BF16),
+            pltpu.VMEM((n_oc, 2, n_out // 2, r_out, o_chunk), BF16),
+            pltpu.VMEM((n_oc, n_out // 2, r_out, o_chunk), BF16),
+            pltpu.VMEM((n_oc, n_out // 2, r_out, o_chunk), BF16),
+            pltpu.VMEM((n_oc, n_out // 2, r_out, o_chunk), BF16),
             pltpu.VMEM((n_blk, rp, 1), F32),
             pltpu.VMEM((n_blk, rp, 1), F32),
             pltpu.VMEM((n_blk, rp, HD), F32),
             dma((2,)), dma((n_qc,)), dma, dma((4,)),
-            dma((n_seq, 4)), dma((n_seq, 4)),
+            dma((n_seq, 4, n_kvh)), dma((n_seq, 4, n_kvh)),
             dma((n_qc, n_ctx)), dma((n_qc, n_ctx)),
-            dma((n_ctx,)), dma((n_ctx,)),
-            dma((n_oc, n_out)), dma((n_oc, n_out)),
+            dma((n_qc, n_ctx)), dma((n_qc, n_ctx)),
+            dma((n_oc,)), dma((n_oc,)),
+            dma((n_oc, n_out // 2)), dma((n_oc, n_out // 2)),
         ],
         compiler_params=pltpu.CompilerParams(
             collective_id=0, has_side_effects=True, vmem_limit_bytes=56 * 1024 * 1024
         ),
-    )(q_new, k_prefix, v_prefix, k_new, v_new, block_offsets, dec_hidden, wq, wo, k_own, v_own, limits)
+    )(q_new, k_prefix, v_prefix, k_new, v_new, block_offsets, dec_hidden, wq, wo, k_own, v_own, valid_len[None], parent[None])
 
 
 def solution(mesh):

time: 65.1 us -> 62.5 us (0.960); the launches traced: 64.9 us -> 61.6 us
  Pallas kernels: 59.3 us -> 57.5 us
  local copies, waits for them, and re-layouts: 4.24 us -> 3.44 us
  other arithmetic: 0.7 us -> 0 us
    pallas_call x1, Pallas kernels: 59.3 us -> 57.5 us  [body(): pl.pallas_call(functools.partial(kernel, (n_seq, n_head, n_ctx, q_chunk,...]
    another operation x1 -> x0, local copies, waits for them, and re-layouts: 0.8 us -> none  [body(): limits = jnp.stack([valid_len, parent], axis=1)]
    another operation x1 -> x0, other arithmetic: 0.7 us -> none  [body(): limits = jnp.stack([valid_len, parent], axis=1)]
where the time goes in v2:
time: 62.5 us; the launch traced here: 61.6 us
  Pallas kernels  57.5 us (92%)
  local copies, waits for them, and re-layouts  3.44 us (6%)
  between operations  0.64 us (1%)
    pallas_call x1, Pallas kernels, body(): pl.pallas_call(functools.partial(kernel, (n_seq, n_head, n_ctx, q_chunk,...  57.5 us
    unnamed x2, local copies, waits for them, and re-layouts  3.44 us

profile of v2, /device:TPU:0, one launch (start us, length us, event | category | flops | bytes accessed | tf_op | source)
XLA Modules:
  0.0 61.6 jit_solution(3927933717509608405)
XLA Ops:
  0.6 57.5 %shard_map.140 = (bf16[512,512]{1,0:T(8,128)(2,1)}, bf16[32,2048]{1,0:T(8,128)(2,1)}) custom-call(bf16[512,512]{1,0:T(8,128)(2,1)} %q_hbm.1, bf16[512,256]{1,0:T(8,128)(2,1)} %kp_hbm.1, bf16[512,256]{1,0:T(8,128)(2,1)} %vp_hbm.1, bf16[512,256]{1,0:T(8,128)(2,1)} %kn_hbm.1, bf16[512,256]{1,0:T(8,128)(2,1)} %vn_hbm.1, s32[4]{0:T(128)} %off_ref.1, ...), custom_call_target="tpu_custom_call" | custom-call | tf_op jit(solution)/shard_map/pallas_call | solution.py:277
  58.1 1.9 %copy.17 = bf16[512,512]{1,0:T(8,128)(2,1)} copy(bf16[512,512]{1,0:T(8,128)(2,1)} %get-tuple-element.4) | data formatting | bytes 1048576
  60.0 1.6 %copy.18 = bf16[32,2048]{1,0:T(8,128)(2,1)} copy(bf16[32,2048]{1,0:T(8,128)(2,1)} %get-tuple-element.5) | data formatting | bytes 262144

commit v3 on v2

--- a/solution.py
+++ b/solution.py
@@ -172,6 +172,18 @@
             state, dq, kv[d, 2, :, lanes_dec], kv[d, 3, :, lanes_dec], tile(pos <= parent, h_chunk)
         )
 
+    def remote_block(b, _):
+        queries = stacked(b)
+        state = lax.fori_loop(
+            1, n_seq, lambda d, st: prefill_step(st, queries, b, d), (m_s[b], l_s[b], a_s[b])
+        )
+        out = (state[2] / state[1]).astype(BF16)
+        tokens = pl.ds(pl.multiple_of(b * QBLK, QBLK), QBLK)
+        for h in range(per_dev):
+            pre_ref[tokens, h * HD:(h + 1) * HD] = out[h * QBLK:(h + 1) * QBLK]
+        return 0
+
+    early = n_blk // 2 if n_qc > 1 else 0
     for c in kv_copies[0]:
         c.wait_recv()
     a_copies = []
@@ -197,17 +209,11 @@
                     {"ctx": lax.rem(ctx + d, n_ctx)},
                 )
             )
-
-    def remote_block(b, _):
-        queries = stacked(b)
-        state = lax.fori_loop(
-            1, n_seq, lambda d, st: prefill_step(st, queries, b, d), (m_s[b], l_s[b], a_s[b])
-        )
-        out = (state[2] / state[1]).astype(BF16)
-        tokens = pl.ds(pl.multiple_of(b * QBLK, QBLK), QBLK)
-        for h in range(per_dev):
-            pre_ref[tokens, h * HD:(h + 1) * HD] = out[h * QBLK:(h + 1) * QBLK]
-        return 0
+        if c == 0:
+            for group in kv_copies[1:]:
+                for copy in group:
+                    copy.wait_recv()
+            lax.fori_loop(0, early, remote_block, 0)
 
     load_wo.wait()
     for c in a_copies:
@@ -241,10 +247,7 @@
             o_copies.append(
                 remote(osum.at[c, t], orecv.at[c, d], o_send.at[c, d], o_recv.at[c, d], to)
             )
-    for group in kv_copies[1:]:
-        for c in group:
-            c.wait_recv()
-    lax.fori_loop(0, n_blk, remote_block, 0)
+    lax.fori_loop(early, n_blk, remote_block, 0)
     for c in range(n_oc):
         acc = osum[c, me_out // 2].astype(F32)
         for d in range(1, n_out // 2):

time: 62.5 us -> 60.7 us (0.971); the launches traced: 61.6 us -> 60.5 us
  Pallas kernels: 57.5 us -> 56.4 us
    pallas_call x1, Pallas kernels: 57.5 us -> 56.4 us  [body(): pl.pallas_call(functools.partial(kernel, (n_seq, n_head, n_ctx, q_chunk,...]
where the time goes in v3:
time: 60.7 us; the launch traced here: 60.5 us
  Pallas kernels  56.4 us (93%)
  local copies, waits for them, and re-layouts  3.44 us (6%)
  between operations  0.64 us (1%)
    pallas_call x1, Pallas kernels, body(): pl.pallas_call(functools.partial(kernel, (n_seq, n_head, n_ctx, q_chunk,...  56.4 us
    unnamed x2, local copies, waits for them, and re-layouts  3.44 us

profile of v3, /device:TPU:0, one launch (start us, length us, event | category | flops | bytes accessed | tf_op | source)
XLA Modules:
  0.0 60.5 jit_solution(3841918990117912244)
XLA Ops:
  0.6 56.4 %shard_map.140 = (bf16[512,512]{1,0:T(8,128)(2,1)}, bf16[32,2048]{1,0:T(8,128)(2,1)}) custom-call(bf16[512,512]{1,0:T(8,128)(2,1)} %q_hbm.1, bf16[512,256]{1,0:T(8,128)(2,1)} %kp_hbm.1, bf16[512,256]{1,0:T(8,128)(2,1)} %vp_hbm.1, bf16[512,256]{1,0:T(8,128)(2,1)} %kn_hbm.1, bf16[512,256]{1,0:T(8,128)(2,1)} %vn_hbm.1, s32[4]{0:T(128)} %off_ref.1, ...), custom_call_target="tpu_custom_call" | custom-call | tf_op jit(solution)/shard_map/pallas_call | solution.py:280
  57.0 1.9 %copy.17 = bf16[512,512]{1,0:T(8,128)(2,1)} copy(bf16[512,512]{1,0:T(8,128)(2,1)} %get-tuple-element.4) | data formatting | bytes 1048576
  58.9 1.6 %copy.18 = bf16[32,2048]{1,0:T(8,128)(2,1)} copy(bf16[32,2048]{1,0:T(8,128)(2,1)} %get-tuple-element.5) | data formatting | bytes 262144
